TPU v7x, 128 devices: a whole 4x4x4 slice. The times are simulated.
128 devices in a mesh: ctx: 16 (over y, x), head: 8 (over z, core).
Axes of the slice: x: 4, y: 4, z: 4, core: 2. Of those that a mesh axis runs over, the one named last changes fastest.
Arguments:
- queries: bfloat16 [32768, 4096], P(('ctx', 'head')), may hold values from -26 to 26
- span_kv: bfloat16 [32768, 2048], P(('ctx', 'head')), may hold values from -6 to 6
- context_kv: bfloat16 [8, 262144, 256], P('head', 'ctx'), may hold values from -6 to 6
- selected: int32 [8, 64, 3], P('head'), may hold values from 0 to 511, as said below
Outputs:
- attended: bfloat16 [32768, 4096], P(('ctx', 'head'))
Inputs may be any that keep to these rules, and one draw needn't show every extreme that they name: `selected`: within one query block the 3 indices differ. For each key-value head and each run of 4 query blocks that one index of ctx holds, at most 2 of their selections lie in one range of 32 context blocks that one index of ctx holds, and exactly 2 in some range.
All inputs are finite; a program needn't handle non-finite values.
Results may differ from a plain program's by a relative error of at most 0.0057.
Values may be sent and summed in bfloat16 or wider, within the bound.
No kernel may reach another device: no remote copies, remote signals or barrier semaphores. Data moves between devices by JAX's collectives and lax.ppermute only.
A program may use at most 192 MiB of HBM per device.

v0:
```python
import jax
import jax.numpy as jnp
import numpy as np
from jax import lax
from jax.experimental import pallas as pl
from jax.experimental.pallas import tpu as pltpu
from jax.sharding import PartitionSpec as P

BLK = 512
CAP = 2
DH = 128
GROUP = 4
TOPK = 3
QB = 4
ENTRIES = QB * TOPK
SIDE = 4
ONES = 16
C = DH ** -0.5 * 1.4426950408889634

ORDER = [
    (0, 1), (0, 3), (1, 0), (3, 0), (2, 2), (1, 1), (3, 3), (1, 3),
    (3, 1), (1, 2), (3, 2), (2, 1), (2, 3), (0, 2), (2, 0),
]
SELF = len(ORDER)
FIRST = 5
GROUPS = [[SELF, 0, 1], [2, 3, 4], [5, 6, 7, 8, 9], [10, 11]]
LAST = [12, 13, 14]
FLIGHT = 5

VMEM = pl.BlockSpec(memory_space=pltpu.VMEM)
SMEM = pl.BlockSpec(memory_space=pltpu.SMEM)
HBM = pl.BlockSpec(memory_space=pltpu.HBM)
WIDE = pltpu.CompilerParams(vmem_limit_bytes=54 * 1024 * 1024)
PARAMS = pltpu.CompilerParams(vmem_limit_bytes=20 * 1024 * 1024)


def place_table(members):
    table = np.full((SIDE * SIDE,), -1, np.int32)
    for place, number in enumerate(members):
        dy, dx = (0, 0) if number == SELF else ORDER[number]
        table[dy * SIDE + dx] = place
    return jnp.asarray(table)


def ctx_position():
    rank = lax.axis_index("ctx")
    return rank // SIDE, rank % SIDE


def serve_start(members, sel_ref, tiles_ref, outs, stage, sem, sem_out):
    y, x = ctx_position()
    me = y * SIDE + x
    copies = []
    for out, number in zip(outs, members):
        dy, dx = (0, 0) if number == SELF else ORDER[number]
        asker = ((y + dy) % SIDE) * SIDE + (x + dx) % SIDE
        found = jnp.int32(0)
        which = [jnp.int32(0)] * CAP
        for e in range(ENTRIES):
            pick = sel_ref[e % TOPK, 0, asker * QB + e // TOPK]
            hit = pick // 32 == me
            for s in range(CAP):
                which[s] = jnp.where(hit & (found == s), pick % 32, which[s])
            found = found + hit.astype(jnp.int32)
        for s in range(CAP):
            place = len(copies)
            if stage is None:
                copies.append(pltpu.make_async_copy(tiles_ref.at[which[s]], out.at[s], sem.at[place]))
                copies[-1].start()
                continue
            copy = pltpu.make_async_copy(tiles_ref.at[which[s]], stage.at[place], sem.at[place])
            copy.start()
            copies.append((copy, pltpu.make_async_copy(stage.at[place], out.at[s], sem_out.at[place])))
    return copies


def pass_on(copies):
    for copy, onward in copies:
        copy.wait()
        onward.start()
    for _, onward in copies:
        onward.wait()


def serve_kernel(members, sel_ref, tiles_ref, *refs):
    pass_on(serve_start(members, sel_ref, tiles_ref, refs[:-3], *refs[-3:]))


def first_kernel(members, heads, sel_ref, tiles_ref, q_ref, s_ref, *refs):
    outs, (packed_ref, sem, q_sem, s_sem) = refs[:-4], refs[-4:]
    width = GROUP * DH
    inward = []
    for h in range(heads):
        inward.append(
            pltpu.make_async_copy(
                q_ref.at[:, pl.ds(h * width, width)], packed_ref.at[h, :, pl.ds(0, width)], q_sem.at[h]
            )
        )
        inward.append(
            pltpu.make_async_copy(
                s_ref.at[:, pl.ds(h * 2 * DH, 2 * DH)], packed_ref.at[h, :, pl.ds(width, 2 * DH)], s_sem.at[h]
            )
        )
    for copy in inward:
        copy.start()
    copies = serve_start(members, sel_ref, tiles_ref, outs, None, sem, None)
    for copy in inward + copies:
        copy.wait()


def stage_shapes(n, dtype):
    return [
        pltpu.VMEM((CAP * n, BLK, 2 * DH), dtype),
        pltpu.SemaphoreType.DMA((CAP * n,)),
        pltpu.SemaphoreType.DMA((CAP * n,)),
    ]


def serve_call(members, sel, tiles):
    n = len(members)
    return pl.pallas_call(
        lambda *refs: serve_kernel(members, *refs),
        in_specs=[SMEM, HBM],
        out_specs=[HBM] * n,
        out_shape=[jax.ShapeDtypeStruct((CAP, BLK, 2 * DH), tiles.dtype)] * n,
        scratch_shapes=stage_shapes(n, tiles.dtype),
        compiler_params=WIDE,
        name="serve",
    )(sel, tiles)


def first_call(members, sel, tiles, queries, span_kv, heads):
    n = len(members)
    packed = (heads, queries.shape[0], (GROUP + 2) * DH)
    return pl.pallas_call(
        lambda *refs: first_kernel(members, heads, *refs),
        in_specs=[SMEM, HBM, HBM, HBM],
        out_specs=[VMEM] * (n + 1),
        out_shape=[jax.ShapeDtypeStruct((CAP, BLK, 2 * DH), tiles.dtype)] * n
        + [jax.ShapeDtypeStruct(packed, queries.dtype)],
        scratch_shapes=[
            pltpu.SemaphoreType.DMA((CAP * n,)),
            pltpu.SemaphoreType.DMA((heads,)),
            pltpu.SemaphoreType.DMA((heads,)),
        ],
        compiler_params=WIDE,
        name="first",
    )(sel, tiles, queries, span_kv)


def values_t(v):
    return jnp.concatenate([v.T, jnp.ones((ONES, BLK), v.dtype)], axis=0)


def scores_t(k, q):
    return lax.dot_general(k, q, (((1,), (1,)), ((), ())), preferred_element_type=jnp.float32)


def own_kernel(x_ref, acc, ml):
    def body(b, carry):
        k = x_ref[b, :, GROUP * DH:(GROUP + 1) * DH]
        vt = values_t(x_ref[b, :, (GROUP + 1) * DH:])
        key = lax.broadcasted_iota(jnp.int32, (BLK, BLK), 0)
        query = lax.broadcasted_iota(jnp.int32, (BLK, BLK), 1)
        found = [scores_t(k, x_ref[b, :, g * DH:(g + 1) * DH]) for g in range(GROUP)]
        for g in range(GROUP):
            s = jnp.where(key <= query, found[g], -jnp.inf)
            m = jnp.max(s, axis=0, keepdims=True)
            p = jnp.exp2((s - m) * C).astype(jnp.bfloat16)
            pv = jnp.dot(vt, p, preferred_element_type=jnp.float32)
            acc[b, g] = pv[:DH]
            ml[b, g, 0:1] = m
            ml[b, g, 1:2] = pv[DH:DH + 1]
        return carry

    lax.fori_loop(0, QB, body, 0)


def add_block(q, kv, acc, ml, at):
    k = kv[:, :DH]
    vt = values_t(kv[:, DH:])
    found = [scores_t(k, q[:, g * DH:(g + 1) * DH]) for g in range(GROUP)]
    for g in range(GROUP):
        s = found[g]
        m_old = ml[at, g, 0:1]
        m = jnp.maximum(m_old, jnp.max(s, axis=0, keepdims=True))
        p = jnp.exp2((s - m) * C).astype(jnp.bfloat16)
        alpha = jnp.exp2((m_old - m) * C)
        pv = jnp.dot(vt, p, preferred_element_type=jnp.float32)
        acc[at, g] = acc[at, g] * alpha + pv[:DH]
        ml[at, g, 0:1] = m
        ml[at, g, 1:2] = ml[at, g, 1:2] * alpha + pv[DH:DH + 1]


def each_arrived(sel_ref, place_ref, x_ref, kv_refs, scratch, first, count, step):
    q_s, kv_s, kv_all, which_s, sem = scratch
    y, x = ctx_position()
    base = (y * SIDE + x) * QB

    def fetch(e, found):
        pick = sel_ref[e % TOPK, 0, base + e // TOPK]
        owner = pick // 32
        slot = jnp.int32(0)
        for f in range(ENTRIES):
            same = (sel_ref[f % TOPK, 0, base + f // TOPK] // 32 == owner) & (f < e)
            slot = slot + same.astype(jnp.int32)
        dy = (y - owner // SIDE + SIDE) % SIDE
        dx = (x - owner % SIDE + SIDE) % SIDE
        place = place_ref[dy * SIDE + dx]
        for i, ref in enumerate(kv_refs):
            @pl.when(place == i)
            def _(ref=ref):
                pltpu.make_async_copy(ref.at[slot], kv_all.at[found], sem.at[found]).start()

        @pl.when(place >= 0)
        def _():
            which_s[found] = e // TOPK

        return found + (place >= 0).astype(jnp.int32)

    def work(n, carry):
        b = which_s[n]
        q_s[...] = x_ref[b, :, :GROUP * DH]
        pltpu.make_async_copy(kv_refs[0].at[0], kv_all.at[n], sem.at[n]).wait()
        kv_s[...] = kv_all[n]
        step(b, q_s, kv_s[...])
        return carry

    lax.fori_loop(0, lax.fori_loop(first, first + count, fetch, jnp.int32(0)), work, 0)


def arrived_scratch(n, dtype):
    return [
        pltpu.VMEM((BLK, GROUP * DH), dtype),
        pltpu.VMEM((BLK, 2 * DH), dtype),
        pltpu.VMEM((n, BLK, 2 * DH), dtype),
        pltpu.SMEM((n,), jnp.int32),
        pltpu.SemaphoreType.DMA((n,)),
    ]


def far_kernel(n, sel_ref, place_ref, x_ref, *refs):
    kv_refs, (acc_in, ml_in, acc, ml), scratch = refs[:n], refs[n:n + 4], refs[n + 4:]
    acc[...] = acc_in[...]
    ml[...] = ml_in[...]
    each_arrived(
        sel_ref, place_ref, x_ref, kv_refs, scratch, 0, ENTRIES,
        lambda b, q, kv: add_block(q, kv, acc, ml, b),
    )


def last_kernel(n, aheads, sel_ref, place_ref, x_ref, *refs):
    kv_refs, refs = refs[:n], refs[n:]
    acc_in, ml_in, refs = refs[0], refs[1], refs[2:]
    outs, (acc, ml, out_s), scratch = refs[:2 * len(aheads)], refs[2 * len(aheads):][:3], refs[2 * len(aheads) + 3:]
    rank = lax.axis_index("head")
    core = rank % 2
    half = BLK // 2
    for i, ahead in enumerate(aheads):
        b = (rank // 2 + ahead) % QB
        acc[0] = acc_in[b]
        ml[0] = ml_in[b]
        each_arrived(
            sel_ref, place_ref, x_ref, kv_refs, scratch, b * TOPK, TOPK,
            lambda b, q, kv: add_block(q, kv, acc, ml, 0),
        )
        for g in range(GROUP):
            out = (acc[0, g] * (1.0 / ml[0, g, 1:2])).astype(out_s.dtype)
            out_s[:, g * DH:(g + 1) * DH] = out.T
        outs[2 * i][...] = out_s[pl.ds(pl.multiple_of(core * half, half), half), :]
        outs[2 * i + 1][...] = out_s[pl.ds(pl.multiple_of((1 - core) * half, half), half), :]


ACC = (QB, GROUP, DH, BLK)
ML = (QB, GROUP, 8, BLK)


def state_shapes():
    return [jax.ShapeDtypeStruct(ACC, jnp.float32), jax.ShapeDtypeStruct(ML, jnp.float32)]


def cost(blocks):
    units = int(blocks * GROUP)
    return pl.CostEstimate(
        flops=units * 4 * BLK * BLK * DH, bytes_accessed=units * BLK * DH * 2, transcendentals=units * BLK * BLK
    )


def own_call(x):
    return pl.pallas_call(
        own_kernel,
        in_specs=[VMEM],
        out_specs=[VMEM, VMEM],
        out_shape=state_shapes(),
        compiler_params=PARAMS,
        cost_estimate=cost(QB),
        name="own_blocks",
    )(x)


def far_call(sel, place, x, tiles, acc, ml):
    n = len(tiles)
    return pl.pallas_call(
        lambda *refs: far_kernel(n, *refs),
        in_specs=[SMEM, SMEM, VMEM] + [HBM] * n + [VMEM] * 2,
        out_specs=[VMEM, VMEM],
        out_shape=state_shapes(),
        scratch_shapes=arrived_scratch(CAP * n, x.dtype),
        compiler_params=PARAMS,
        cost_estimate=cost(n * 0.75),
        name="far_blocks",
    )(sel, place, x, *tiles, acc, ml)


def last_call(aheads, sel, place, x, tiles, acc, ml):
    n = len(tiles)
    half = BLK // 2
    return pl.pallas_call(
        lambda *refs: last_kernel(n, aheads, *refs),
        in_specs=[SMEM, SMEM, VMEM] + [HBM] * n + [VMEM] * 2,
        out_specs=[VMEM] * (2 * len(aheads)),
        out_shape=[jax.ShapeDtypeStruct((half, GROUP * DH), x.dtype)] * (2 * len(aheads)),
        scratch_shapes=[
            pltpu.VMEM((1,) + ACC[1:], jnp.float32),
            pltpu.VMEM((1,) + ML[1:], jnp.float32),
            pltpu.VMEM((BLK, GROUP * DH), x.dtype),
        ] + arrived_scratch(TOPK, x.dtype),
        compiler_params=PARAMS,
        cost_estimate=cost(1),
        name="last_blocks",
    )(sel, place, x, *tiles, acc, ml)


def assemble_kernel(steps, *refs):
    pieces, out_ref = refs[:-1], refs[-1]
    rank = lax.axis_index("head")
    z, core = rank // 2, rank % 2
    width = GROUP * DH
    for (dz, dc), piece in zip(steps, pieces):
        sender = ((z - dz + QB) % QB) * 2 + (core + dc) % 2
        out_ref[:, pl.ds(pl.multiple_of(sender * width, width), width)] = piece[...]


def assemble_call(steps, pieces, heads):
    rows, width = pieces[0].shape
    return pl.pallas_call(
        lambda *refs: assemble_kernel(steps, *refs),
        in_specs=[VMEM] * len(pieces),
        out_specs=VMEM,
        out_shape=jax.ShapeDtypeStruct((rows, heads * width), pieces[0].dtype),
        compiler_params=PARAMS,
        name="assemble",
    )(*pieces)


def ctx_shift(value, dy, dx):
    pairs = [
        (y * SIDE + x, ((y + dy) % SIDE) * SIDE + (x + dx) % SIDE) for y in range(SIDE) for x in range(SIDE)
    ]
    return lax.ppermute(value, "ctx", pairs)


def head_shift(value, dz, dc):
    pairs = [(z * 2 + c, ((z + dz) % QB) * 2 + (c + dc) % 2) for z in range(QB) for c in range(2)]
    return lax.ppermute(value, "head", pairs)


def local(queries, span_kv, context_kv, selected):
    heads = lax.axis_size("head")
    rows = queries.shape[0]
    sel = selected.transpose(2, 0, 1)
    stored = context_kv[0]
    tiles = stored.reshape(stored.shape[0] // BLK, BLK, 2 * DH)

    numbers = list(range(SELF + 1))
    *begin, packed = first_call(numbers[:FIRST], sel, tiles, queries, span_kv, heads)
    sent = dict(zip(numbers[:FIRST], begin))
    sent.update(zip(numbers[FIRST:], serve_call(numbers[FIRST:], sel, tiles)))
    x = lax.all_to_all(packed, "head", split_axis=0, concat_axis=0, tiled=True)
    x = x.reshape(QB, heads * rows // QB, (GROUP + 2) * DH)

    arrived = {SELF: sent[SELF]}

    def send(number, *before):
        value = sent[number]
        if number >= FLIGHT:
            value, arrived[number - FLIGHT], *before = lax.optimization_barrier(
                (value, arrived[number - FLIGHT], *before)
            )
        arrived[number] = ctx_shift(value, *ORDER[number])
        return before

    def far(members, acc, ml):
        return far_call(sel, place_table(members), x, [arrived[i] for i in members], acc, ml)

    for number in range(2 * FLIGHT):
        send(number)
    acc, ml = own_call(x)
    for number in (10, 11):
        ml, = send(number, ml)
    acc, ml = far(GROUPS[0], acc, ml)
    for number in (12, 13):
        ml, = send(number, ml)
    acc, ml = far(GROUPS[1], acc, ml)
    ml, = send(14, ml)
    for members in GROUPS[2:]:
        acc, ml = far(members, acc, ml)

    ready = {}
    for aheads in ((2,), (1, 3, 0)):
        outs = last_call(aheads, sel, place_table(LAST), x, [arrived[i] for i in LAST], acc, ml)
        *outs, acc = lax.optimization_barrier((*outs, acc))
        for i, dz in enumerate(aheads):
            for dc in range(2):
                ready[dz, dc] = outs[2 * i + dc]
    steps = [(2, 0), (2, 1), (1, 0), (3, 0), (1, 1), (3, 1), (0, 1)]
    pieces = []
    for number, step in enumerate(steps):
        value = ready[step]
        if number >= FLIGHT:
            value, pieces[number - FLIGHT] = lax.optimization_barrier((value, pieces[number - FLIGHT]))
        pieces.append(head_shift(value, *step))
    steps.append((0, 0))
    pieces.append(ready[0, 0])
    return assemble_call(steps, pieces, heads)


def solution(mesh):
    placed = (
        P(("ctx", "head"), None),
        P(("ctx", "head"), None),
        P("head", "ctx", None),
        P("head", None, None),
    )
    return jax.shard_map(
        local, mesh=mesh, in_specs=placed, out_specs=P(("ctx", "head"), None), check_vma=False
    )
```

profile of v0, /device:TPU:25, one launch (start us, length us, event | category | flops | bytes accessed | tf_op | source)
XLA Modules:
  0.0 158.6 jit_solution(7603227542604884627)
XLA Ops:
  0.0 6.2 %first.1 = (bf16[2,512,256]{2,1,0:T(8,128)(2,1)}, bf16[2,512,256]{2,1,0:T(8,128)(2,1)}, bf16[2,512,256]{2,1,0:T(8,128)(2,1)}, bf16[2,512,256]{2,1,0:T(8,128)(2,1...) custom-call(s32[3,1,64]{2,1,0:T(1,128)} %bitcast.10, bf16[32,512,256]{2,1,0:T(8,128)(2,1)} %bitcast.18, ...), custom_call_target="tpu_custom_call" | custom-call | tf_op jit(solution)/shard_map/first/pallas_call | solution.py:135
  6.2 6.0 %all-to-all-start = ((bf16[8,256,768]{2,1,0:T(8,128)(2,1)}), bf16[8,256,768]{2,1,0:T(8,128)(2,1)S(1)}, u32[]{:S(2)}, u32[]{:S(2)}) async-start(bf16[8,256,768]{2,1,0:T(8,128)(2,1)} %get-tuple-element.78), calls=%async_computation | async-start | bytes 6291456 | tf_op jit(solution)/shard_map/all_to_all | solution.py:379
  16.4 2.5 %collective-permute-start.10 = (bf16[2,512,256]{2,1,0:T(8,128)(2,1)}, bf16[2,512,256]{2,1,0:T(8,128)(2,1)S(1)}, u32[]{:S(2)}, u32[]{:S(2)}) collective-permute-start(bf16[2,512,256]{2,1,0:T(8,128)(2,1)} %get-tuple-element.108), channel_id=1, source_target_pairs={{0,80},{8,88},{16,64},{24,72},{32,112},{40,120},{48,96},{56,104},{... | collective-permute-start | bytes 1572872 | tf_op jit(solution)/shard_map/ppermute | solution.py:360
  18.9 7.1 %serve.1 = (bf16[2,512,256]{2,1,0:T(8,128)(2,1)}, bf16[2,512,256]{2,1,0:T(8,128)(2,1)}, bf16[2,512,256]{2,1,0:T(8,128)(2,1)}, bf16[2,512,256]{2,1,0:T(8,128)(2,1...) custom-call(s32[3,1,64]{2,1,0:T(1,128)} %bitcast.11, ...), custom_call_target="tpu_custom_call" | custom-call | tf_op jit(solution)/shard_map/serve/pallas_call | solution.py:121
  29.4 3.0 %collective-permute-start.4 = (bf16[2,512,256]{2,1,0:T(8,128)(2,1)}, bf16[2,512,256]{2,1,0:T(8,128)(2,1)}, u32[]{:S(2)}, u32[]{:S(2)}) collective-permute-start(bf16[2,512,256]{2,1,0:T(8,128)(2,1)} %get-tuple-element.92), channel_id=1, source_target_pairs={{0,120},{8,96},{16,104},{24,112},{32,24},{40,0},{48,8},{56,16},{64... | collective-permute-start | bytes 1572872 | tf_op jit(solution)/shard_map/ppermute | solution.py:360
  36.4 5.2 %collective-permute-done.10.refs_5_ = bf16[2,512,256]{2,1,0:T(8,128)(2,1)S(1)} collective-permute-done((bf16[2,512,256]{2,1,0:T(8,128)(2,1)}, bf16[2,512,256]{2,1,0:T(8,128)(2,1)S(1)}, u32[]{:S(2)}, u32[]{:S(2)}) %collective-permute-start.10) | collective-permute-done | bytes 524320 | tf_op jit(solution)/shard_map/ppermute | solution.py:360
  42.4 11.2 %collective-permute-start.11 = (bf16[2,512,256]{2,1,0:T(8,128)(2,1)}, bf16[2,512,256]{2,1,0:T(8,128)(2,1)}, u32[]{:S(2)}, u32[]{:S(2)}) collective-permute-start(bf16[2,512,256]{2,1,0:T(8,128)(2,1)} %get-tuple-element.109), channel_id=1, source_target_pairs={{0,48},{8,56},{16,32},{24,40},{32,80},{40,88},{48,64},{56,72},{64,... | collective-permute-start | bytes 1572872 | tf_op jit(solution)/shard_map/ppermute | solution.py:360
  53.7 4.4 %own_blocks.1 = (f32[4,4,128,512]{3,2,1,0:T(8,128)S(1)}, f32[4,4,8,512]{3,2,1,0:T(8,128)S(1)}) custom-call(bf16[4,512,768]{2,1,0:T(8,128)(2,1)S(1)} %bitcast.3), custom_call_target="tpu_custom_call" | custom-call | flops 2147483648 | bytes 2097152 | tf_op jit(solution)/shard_map/own_blocks/pallas_call | solution.py:290
  58.0 4.4 %collective-permute-start.14 = (bf16[2,512,256]{2,1,0:T(8,128)(2,1)S(1)}, bf16[2,512,256]{2,1,0:T(8,128)(2,1)S(1)}, u32[]{:S(2)}, u32[]{:S(2)}) collective-permute-start(bf16[2,512,256]{2,1,0:T(8,128)(2,1)S(1)} %copy-done.21), channel_id=1, source_target_pairs={{0,72},{8,80},{16,88},{24,64},{32,104},{40,112},{48,120},{56,96},{... | collective-permute-start | bytes 1572872 | tf_op jit(solution)/shard_map/ppermute | solution.py:360
  62.6 3.9 %far_blocks.4 = (f32[4,4,128,512]{3,2,1,0:T(8,128)S(1)}, f32[4,4,8,512]{3,2,1,0:T(8,128)S(1)}) custom-call(s32[3,1,64]{2,1,0:T(1,128)S(1)} %bitcast.12, s32[16]{0:T(128)S(1)} %copy-done.16, bf16[4,512,768]{2,1,0:T(8,128)(2,1)S(1)} %bitcast.4, bf16[2,512,256]{2,1,0:T(8,128)(2,1)S(1)} %copy-done.10, bf16[2,512,256]{2,1,0:T(8,128)(2,1)S(1)} %copy-done.7, ...), custom_call_target="tpu_custom_call" | custom-call | flops 1207959552 | bytes 1179648 | tf_op jit(solution)/shard_map/far_blocks/pallas_call | solution.py:303
  66.7 2.5 %far_blocks.5 = (f32[4,4,128,512]{3,2,1,0:T(8,128)S(1)}, f32[4,4,8,512]{3,2,1,0:T(8,128)S(1)}) custom-call(s32[3,1,64]{2,1,0:T(1,128)S(1)} %bitcast.13, s32[16]{0:T(128)S(1)} %copy-done.15, bf16[4,512,768]{2,1,0:T(8,128)(2,1)S(1)} %bitcast.5, bf16[2,512,256]{2,1,0:T(8,128)(2,1)S(1)} %copy-done.1, bf16[2,512,256]{2,1,0:T(8,128)(2,1)S(1)} %copy-done.3, ...), custom_call_target="tpu_custom_call" | custom-call | flops 1207959552 | bytes 1179648 | tf_op jit(solution)/shard_map/far_blocks/pallas_call | solution.py:303
  69.1 6.8 %collective-permute-done.11.refs_7_ = bf16[2,512,256]{2,1,0:T(8,128)(2,1)} collective-permute-done((bf16[2,512,256]{2,1,0:T(8,128)(2,1)}, bf16[2,512,256]{2,1,0:T(8,128)(2,1)}, u32[]{:S(2)}, u32[]{:S(2)}) %collective-permute-start.11) | collective-permute-done | bytes 524320 | tf_op jit(solution)/shard_map/ppermute | solution.py:360
  75.9 5.0 %collective-permute-start.12 = (bf16[2,512,256]{2,1,0:T(8,128)(2,1)S(1)}, bf16[2,512,256]{2,1,0:T(8,128)(2,1)S(1)}, u32[]{:S(2)}, u32[]{:S(2)}) collective-permute-start(bf16[2,512,256]{2,1,0:T(8,128)(2,1)S(1)} %copy-done.19), channel_id=1, source_target_pairs={{0,64},{8,72},{16,80},{24,88},{32,96},{40,104},{48,112},{56,120},{... | collective-permute-start | bytes 1572872 | tf_op jit(solution)/shard_map/ppermute | solution.py:360
  81.5 6.5 %collective-permute-start.6 = (bf16[2,512,256]{2,1,0:T(8,128)(2,1)S(1)}, bf16[2,512,256]{2,1,0:T(8,128)(2,1)S(1)}, u32[]{:S(2)}, u32[]{:S(2)}) collective-permute-start(bf16[2,512,256]{2,1,0:T(8,128)(2,1)S(1)} %copy-done.17), channel_id=1, source_target_pairs={{0,88},{8,64},{16,72},{24,80},{32,120},{40,96},{48,104},{56,112},{... | collective-permute-start | bytes 1572872 | tf_op jit(solution)/shard_map/ppermute | solution.py:360
  87.9 11.1 %far_blocks.6 = (f32[4,4,128,512]{3,2,1,0:T(8,128)S(1)}, f32[4,4,8,512]{3,2,1,0:T(8,128)S(1)}) custom-call(s32[3,1,64]{2,1,0:T(1,128)S(1)} %bitcast.14, s32[16]{0:T(128)S(1)} %copy-done.14, bf16[4,512,768]{2,1,0:T(8,128)(2,1)S(1)} %bitcast.6, bf16[2,512,256]{2,1,0:T(8,128)(2,1)} %collective-permute-done.5.refs_3_, ...), custom_call_target="tpu_custom_call" | custom-call | flops 2013265920 | bytes 1966080 | tf_op jit(solution)/shard_map/far_blocks/pallas_call | solution.py:303
  99.1 3.8 %far_blocks.7 = (f32[4,4,128,512]{3,2,1,0:T(8,128)S(1)}, f32[4,4,8,512]{3,2,1,0:T(8,128)S(1)}) custom-call(s32[3,1,64]{2,1,0:T(1,128)S(1)} %bitcast.15, s32[16]{0:T(128)S(1)} %copy-done.13, bf16[4,512,768]{2,1,0:T(8,128)(2,1)S(1)} %bitcast.7, bf16[2,512,256]{2,1,0:T(8,128)(2,1)S(1)} %collective-permute-done.13.refs_3_, ...), custom_call_target="tpu_custom_call" | custom-call | flops 805306368 | bytes 786432 | tf_op jit(solution)/shard_map/far_blocks/pallas_call | solution.py:303
  102.9 24.6 %collective-permute-done.12.refs_5_ = bf16[2,512,256]{2,1,0:T(8,128)(2,1)S(1)} collective-permute-done((bf16[2,512,256]{2,1,0:T(8,128)(2,1)S(1)}, bf16[2,512,256]{2,1,0:T(8,128)(2,1)S(1)}, u32[]{:S(2)}, u32[]{:S(2)}) %collective-permute-start.12) | collective-permute-done | bytes 524320 | tf_op jit(solution)/shard_map/ppermute | solution.py:360
  127.5 2.8 %last_blocks.2 = (bf16[256,512]{1,0:T(8,128)(2,1)S(1)}, bf16[256,512]{1,0:T(8,128)(2,1)S(1)}) custom-call(s32[3,1,64]{2,1,0:T(1,128)S(1)} %bitcast.16, s32[16]{0:T(128)S(1)} %copy-done.12, bf16[4,512,768]{2,1,0:T(8,128)(2,1)S(1)} %bitcast.8, bf16[2,512,256]{2,1,0:T(8,128)(2,1)S(1)} %collective-permute-done.6.refs_3_, ...), custom_call_target="tpu_custom_call" | custom-call | flops 536870912 | bytes 524288 | tf_op jit(solution)/shard_map/last_blocks/pallas_call | solution.py:318
  130.4 3.6 %collective-permute-start.16 = (bf16[256,512]{1,0:T(8,128)(2,1)S(1)}, bf16[256,512]{1,0:T(8,128)(2,1)S(1)}, u32[]{:S(2)}, u32[]{:S(2)}) collective-permute-start(bf16[256,512]{1,0:T(8,128)(2,1)S(1)} %get-tuple-element.143), channel_id=1, source_target_pairs={{0,5},{1,4},{2,7},{3,6},{4,1},{5,0},{6,3},{7,2},{8,13},{9,12},{10,... | collective-permute-start | bytes 786440 | tf_op jit(solution)/shard_map/ppermute | solution.py:365
  134.0 7.2 %last_blocks.3 = (bf16[256,512]{1,0:T(8,128)(2,1)S(1)}, bf16[256,512]{1,0:T(8,128)(2,1)S(1)}, bf16[256,512]{1,0:T(8,128)(2,1)S(1)}, bf16[256,512]{1,0:T(8,128)(2...) custom-call(s32[3,1,64]{2,1,0:T(1,128)S(1)} %bitcast.17, s32[16]{0:T(128)S(1)} %copy-done.12, ...), custom_call_target="tpu_custom_call" | custom-call | flops 536870912 | bytes 524288 | tf_op jit(solution)/shard_map/last_blocks/pallas_call | solution.py:318
  141.3 2.7 %collective-permute-start.18 = (bf16[256,512]{1,0:T(8,128)(2,1)S(1)}, bf16[256,512]{1,0:T(8,128)(2,1)S(1)}, u32[]{:S(2)}, u32[]{:S(2)}) collective-permute-start(bf16[256,512]{1,0:T(8,128)(2,1)S(1)} %get-tuple-element.146), channel_id=1, source_target_pairs={{0,6},{1,7},{2,0},{3,1},{4,2},{5,3},{6,4},{7,5},{8,14},{9,15},{10,... | collective-permute-start | bytes 786440 | tf_op jit(solution)/shard_map/ppermute | solution.py:365
  143.9 3.0 %collective-permute-start.20 = (bf16[256,512]{1,0:T(8,128)(2,1)S(1)}, bf16[256,512]{1,0:T(8,128)(2,1)S(1)}, u32[]{:S(2)}, u32[]{:S(2)}) collective-permute-start(bf16[256,512]{1,0:T(8,128)(2,1)S(1)} %get-tuple-element.148), channel_id=1, source_target_pairs={{0,7},{1,6},{2,1},{3,0},{4,3},{5,2},{6,5},{7,4},{8,15},{9,14},{10,... | collective-permute-start | bytes 786440 | tf_op jit(solution)/shard_map/ppermute | solution.py:365
  147.2 4.3 %collective-permute-done.17.refs_2_ = bf16[256,512]{1,0:T(8,128)(2,1)S(1)} collective-permute-done((bf16[256,512]{1,0:T(8,128)(2,1)S(1)}, bf16[256,512]{1,0:T(8,128)(2,1)S(1)}, u32[]{:S(2)}, u32[]{:S(2)}) %collective-permute-start.17) | collective-permute-done | bytes 262176 | tf_op jit(solution)/shard_map/ppermute | solution.py:365
  151.5 5.6 %collective-permute-done.19.refs_4_ = bf16[256,512]{1,0:T(8,128)(2,1)S(1)} collective-permute-done((bf16[256,512]{1,0:T(8,128)(2,1)S(1)}, bf16[256,512]{1,0:T(8,128)(2,1)S(1)}, u32[]{:S(2)}, u32[]{:S(2)}) %collective-permute-start.19) | collective-permute-done | bytes 262176 | tf_op jit(solution)/shard_map/ppermute | solution.py:365
  (76 shorter events, 15.1 us)
Async XLA Ops:
  6.2 47.4 %all-to-all-start = ((bf16[8,256,768]{2,1,0:T(8,128)(2,1)}), bf16[8,256,768]{2,1,0:T(8,128)(2,1)S(1)}, u32[]{:S(2)}, u32[]{:S(2)}) async-start(bf16[8,256,768]{2,1,0:T(8,128)(2,1)} %get-tuple-element.78), calls=%async_computation | async-start | bytes 6291456 | tf_op jit(solution)/shard_map/all_to_all | solution.py:379
  12.2 15.0 %collective-permute-start.2 = (bf16[2,512,256]{2,1,0:T(8,128)(2,1)}, bf16[2,512,256]{2,1,0:T(8,128)(2,1)S(1)}, u32[]{:S(2)}, u32[]{:S(2)}) collective-permute-start(bf16[2,512,256]{2,1,0:T(8,128)(2,1)} %get-tuple-element.85), channel_id=1, source_target_pairs={{0,8},{8,16},{16,24},{24,0},{32,40},{40,48},{48,56},{56,32},{64,72... | collective-permute-start | bytes 1572872 | tf_op jit(solution)/shard_map/ppermute | solution.py:360
  13.7 14.9 %collective-permute-start.3 = (bf16[2,512,256]{2,1,0:T(8,128)(2,1)}, bf16[2,512,256]{2,1,0:T(8,128)(2,1)S(1)}, u32[]{:S(2)}, u32[]{:S(2)}) collective-permute-start(bf16[2,512,256]{2,1,0:T(8,128)(2,1)} %get-tuple-element.88), channel_id=1, source_target_pairs={{0,24},{8,0},{16,8},{24,16},{32,56},{40,32},{48,40},{56,48},{64,88... | collective-permute-start | bytes 1572872 | tf_op jit(solution)/shard_map/ppermute | solution.py:360
  14.9 17.6 %collective-permute-start = (bf16[2,512,256]{2,1,0:T(8,128)(2,1)}, bf16[2,512,256]{2,1,0:T(8,128)(2,1)S(1)}, u32[]{:S(2)}, u32[]{:S(2)}) collective-permute-start(bf16[2,512,256]{2,1,0:T(8,128)(2,1)} %get-tuple-element.81), channel_id=1, source_target_pairs={{0,32},{8,40},{16,48},{24,56},{32,64},{40,72},{48,80},{56,88},{64,... | collective-permute-start | bytes 1572872 | tf_op jit(solution)/shard_map/ppermute | solution.py:360
  14.9 19.5 %collective-permute-start.7 = (bf16[2,512,256]{2,1,0:T(8,128)(2,1)}, bf16[2,512,256]{2,1,0:T(8,128)(2,1)S(1)}, u32[]{:S(2)}, u32[]{:S(2)}) collective-permute-start(bf16[2,512,256]{2,1,0:T(8,128)(2,1)} %get-tuple-element.102), channel_id=1, source_target_pairs={{0,96},{8,104},{16,112},{24,120},{32,0},{40,8},{48,16},{56,24},{64... | collective-permute-start | bytes 1572872 | tf_op jit(solution)/shard_map/ppermute | solution.py:360
  16.4 25.2 %collective-permute-start.10 = (bf16[2,512,256]{2,1,0:T(8,128)(2,1)}, bf16[2,512,256]{2,1,0:T(8,128)(2,1)S(1)}, u32[]{:S(2)}, u32[]{:S(2)}) collective-permute-start(bf16[2,512,256]{2,1,0:T(8,128)(2,1)} %get-tuple-element.108), channel_id=1, source_target_pairs={{0,80},{8,88},{16,64},{24,72},{32,112},{40,120},{48,96},{56,104},{... | collective-permute-start | bytes 1572872 | tf_op jit(solution)/shard_map/ppermute | solution.py:360
  25.9 36.6 %copy-start.11 = (s32[1,64,3]{1,0,2:T(1,128)S(1)}, s32[1,64,3]{1,0,2:T(1,128)}, u32[]{:S(2)}) copy-start(s32[1,64,3]{1,0,2:T(1,128)} %param.13) | copy-start | bytes 2308
  28.0 30.0 %collective-permute-start.5 = (bf16[2,512,256]{2,1,0:T(8,128)(2,1)}, bf16[2,512,256]{2,1,0:T(8,128)(2,1)}, u32[]{:S(2)}, u32[]{:S(2)}) collective-permute-start(bf16[2,512,256]{2,1,0:T(8,128)(2,1)} %get-tuple-element.94), channel_id=1, source_target_pairs={{0,40},{8,48},{16,56},{24,32},{32,72},{40,80},{48,88},{56,64},{64,... | collective-permute-start | bytes 1572872 | tf_op jit(solution)/shard_map/ppermute | solution.py:360
  29.4 28.6 %collective-permute-start.4 = (bf16[2,512,256]{2,1,0:T(8,128)(2,1)}, bf16[2,512,256]{2,1,0:T(8,128)(2,1)}, u32[]{:S(2)}, u32[]{:S(2)}) collective-permute-start(bf16[2,512,256]{2,1,0:T(8,128)(2,1)} %get-tuple-element.92), channel_id=1, source_target_pairs={{0,120},{8,96},{16,104},{24,112},{32,24},{40,0},{48,8},{56,16},{64... | collective-permute-start | bytes 1572872 | tf_op jit(solution)/shard_map/ppermute | solution.py:360
  33.3 33.3 %collective-permute-start.1 = (bf16[2,512,256]{2,1,0:T(8,128)(2,1)}, bf16[2,512,256]{2,1,0:T(8,128)(2,1)}, u32[]{:S(2)}, u32[]{:S(2)}) collective-permute-start(bf16[2,512,256]{2,1,0:T(8,128)(2,1)} %get-tuple-element.82), channel_id=1, source_target_pairs={{0,56},{8,32},{16,40},{24,48},{32,88},{40,64},{48,72},{56,80},{64,... | collective-permute-start | bytes 1572872 | tf_op jit(solution)/shard_map/ppermute | solution.py:360
  35.2 31.4 %collective-permute-start.8 = (bf16[2,512,256]{2,1,0:T(8,128)(2,1)}, bf16[2,512,256]{2,1,0:T(8,128)(2,1)}, u32[]{:S(2)}, u32[]{:S(2)}) collective-permute-start(bf16[2,512,256]{2,1,0:T(8,128)(2,1)} %get-tuple-element.103), channel_id=1, source_target_pairs={{0,104},{8,112},{16,120},{24,96},{32,8},{40,16},{48,24},{56,0},{64... | collective-permute-start | bytes 1572872 | tf_op jit(solution)/shard_map/ppermute | solution.py:360
  42.4 33.5 %collective-permute-start.11 = (bf16[2,512,256]{2,1,0:T(8,128)(2,1)}, bf16[2,512,256]{2,1,0:T(8,128)(2,1)}, u32[]{:S(2)}, u32[]{:S(2)}) collective-permute-start(bf16[2,512,256]{2,1,0:T(8,128)(2,1)} %get-tuple-element.109), channel_id=1, source_target_pairs={{0,48},{8,56},{16,32},{24,40},{32,80},{40,88},{48,64},{56,72},{64,... | collective-permute-start | bytes 1572872 | tf_op jit(solution)/shard_map/ppermute | solution.py:360
  58.0 41.0 %collective-permute-start.14 = (bf16[2,512,256]{2,1,0:T(8,128)(2,1)S(1)}, bf16[2,512,256]{2,1,0:T(8,128)(2,1)S(1)}, u32[]{:S(2)}, u32[]{:S(2)}) collective-permute-start(bf16[2,512,256]{2,1,0:T(8,128)(2,1)S(1)} %copy-done.21), channel_id=1, source_target_pairs={{0,72},{8,80},{16,88},{24,64},{32,104},{40,112},{48,120},{56,96},{... | collective-permute-start | bytes 1572872 | tf_op jit(solution)/shard_map/ppermute | solution.py:360
  62.4 36.6 %collective-permute-start.13 = (bf16[2,512,256]{2,1,0:T(8,128)(2,1)S(1)}, bf16[2,512,256]{2,1,0:T(8,128)(2,1)S(1)}, u32[]{:S(2)}, u32[]{:S(2)}) collective-permute-start(bf16[2,512,256]{2,1,0:T(8,128)(2,1)S(1)} %copy-done.20), channel_id=1, source_target_pairs={{0,112},{8,120},{16,96},{24,104},{32,16},{40,24},{48,0},{56,8},{64... | collective-permute-start | bytes 1572872 | tf_op jit(solution)/shard_map/ppermute | solution.py:360
  75.9 51.5 %collective-permute-start.12 = (bf16[2,512,256]{2,1,0:T(8,128)(2,1)S(1)}, bf16[2,512,256]{2,1,0:T(8,128)(2,1)S(1)}, u32[]{:S(2)}, u32[]{:S(2)}) collective-permute-start(bf16[2,512,256]{2,1,0:T(8,128)(2,1)S(1)} %copy-done.19), channel_id=1, source_target_pairs={{0,64},{8,72},{16,80},{24,88},{32,96},{40,104},{48,112},{56,120},{... | collective-permute-start | bytes 1572872 | tf_op jit(solution)/shard_map/ppermute | solution.py:360
  80.9 46.5 %collective-permute-start.9 = (bf16[2,512,256]{2,1,0:T(8,128)(2,1)S(1)}, bf16[2,512,256]{2,1,0:T(8,128)(2,1)S(1)}, u32[]{:S(2)}, u32[]{:S(2)}) collective-permute-start(bf16[2,512,256]{2,1,0:T(8,128)(2,1)S(1)} %copy-done.18), channel_id=1, source_target_pairs={{0,16},{8,24},{16,0},{24,8},{32,48},{40,56},{48,32},{56,40},{64,80... | collective-permute-start | bytes 1572872 | tf_op jit(solution)/shard_map/ppermute | solution.py:360
  81.5 46.0 %collective-permute-start.6 = (bf16[2,512,256]{2,1,0:T(8,128)(2,1)S(1)}, bf16[2,512,256]{2,1,0:T(8,128)(2,1)S(1)}, u32[]{:S(2)}, u32[]{:S(2)}) collective-permute-start(bf16[2,512,256]{2,1,0:T(8,128)(2,1)S(1)} %copy-done.17), channel_id=1, source_target_pairs={{0,88},{8,64},{16,72},{24,80},{32,120},{40,96},{48,104},{56,112},{... | collective-permute-start | bytes 1572872 | tf_op jit(solution)/shard_map/ppermute | solution.py:360
  130.3 13.6 %collective-permute-start.15 = (bf16[256,512]{1,0:T(8,128)(2,1)S(1)}, bf16[256,512]{1,0:T(8,128)(2,1)S(1)}, u32[]{:S(2)}, u32[]{:S(2)}) collective-permute-start(bf16[256,512]{1,0:T(8,128)(2,1)S(1)} %get-tuple-element.140), channel_id=1, source_target_pairs={{0,4},{1,5},{2,6},{3,7},{4,0},{5,1},{6,2},{7,3},{8,12},{9,13},{10,... | collective-permute-start | bytes 786440 | tf_op jit(solution)/shard_map/ppermute | solution.py:365
  130.4 16.5 %collective-permute-start.16 = (bf16[256,512]{1,0:T(8,128)(2,1)S(1)}, bf16[256,512]{1,0:T(8,128)(2,1)S(1)}, u32[]{:S(2)}, u32[]{:S(2)}) collective-permute-start(bf16[256,512]{1,0:T(8,128)(2,1)S(1)} %get-tuple-element.143), channel_id=1, source_target_pairs={{0,5},{1,4},{2,7},{3,6},{4,1},{5,0},{6,3},{7,2},{8,13},{9,12},{10,... | collective-permute-start | bytes 786440 | tf_op jit(solution)/shard_map/ppermute | solution.py:365
  141.2 10.3 %collective-permute-start.17 = (bf16[256,512]{1,0:T(8,128)(2,1)S(1)}, bf16[256,512]{1,0:T(8,128)(2,1)S(1)}, u32[]{:S(2)}, u32[]{:S(2)}) collective-permute-start(bf16[256,512]{1,0:T(8,128)(2,1)S(1)} %get-tuple-element.145), channel_id=1, source_target_pairs={{0,2},{1,3},{2,4},{3,5},{4,6},{5,7},{6,0},{7,1},{8,10},{9,11},{10,... | collective-permute-start | bytes 786440 | tf_op jit(solution)/shard_map/ppermute | solution.py:365
  141.3 10.2 %collective-permute-start.18 = (bf16[256,512]{1,0:T(8,128)(2,1)S(1)}, bf16[256,512]{1,0:T(8,128)(2,1)S(1)}, u32[]{:S(2)}, u32[]{:S(2)}) collective-permute-start(bf16[256,512]{1,0:T(8,128)(2,1)S(1)} %get-tuple-element.146), channel_id=1, source_target_pairs={{0,6},{1,7},{2,0},{3,1},{4,2},{5,3},{6,4},{7,5},{8,14},{9,15},{10,... | collective-permute-start | bytes 786440 | tf_op jit(solution)/shard_map/ppermute | solution.py:365
  143.9 13.2 %collective-permute-start.19 = (bf16[256,512]{1,0:T(8,128)(2,1)S(1)}, bf16[256,512]{1,0:T(8,128)(2,1)S(1)}, u32[]{:S(2)}, u32[]{:S(2)}) collective-permute-start(bf16[256,512]{1,0:T(8,128)(2,1)S(1)} %get-tuple-element.147), channel_id=1, source_target_pairs={{0,3},{1,2},{2,5},{3,4},{4,7},{5,6},{6,1},{7,0},{8,11},{9,10},{10,... | collective-permute-start | bytes 786440 | tf_op jit(solution)/shard_map/ppermute | solution.py:365
  143.9 13.2 %collective-permute-start.20 = (bf16[256,512]{1,0:T(8,128)(2,1)S(1)}, bf16[256,512]{1,0:T(8,128)(2,1)S(1)}, u32[]{:S(2)}, u32[]{:S(2)}) collective-permute-start(bf16[256,512]{1,0:T(8,128)(2,1)S(1)} %get-tuple-element.148), channel_id=1, source_target_pairs={{0,7},{1,6},{2,1},{3,0},{4,3},{5,2},{6,5},{7,4},{8,15},{9,14},{10,... | collective-permute-start | bytes 786440 | tf_op jit(solution)/shard_map/ppermute | solution.py:365
  146.9 10.2 %collective-permute-start.21 = (bf16[256,512]{1,0:T(8,128)(2,1)S(1)}, bf16[256,512]{1,0:T(8,128)(2,1)S(1)}, u32[]{:S(2)}, u32[]{:S(2)}) collective-permute-start(bf16[256,512]{1,0:T(8,128)(2,1)S(1)} %get-tuple-element.149), channel_id=1, source_target_pairs={{0,1},{1,0},{2,3},{3,2},{4,5},{5,4},{6,7},{7,6},{8,9},{9,8},{10,11... | collective-permute-start | bytes 786440 | tf_op jit(solution)/shard_map/ppermute | solution.py:365
  (21 other events, 195.9 us)
where the time goes:
time: 160 us; the launch traced here: 159 us
  starting transfers between devices  55.9 us (35%)
  Pallas kernels  50.4 us (32%)
  waiting for transfers between devices  47.8 us (30%)
  local copies, waits for them, and re-layouts  4.16 us (3%)
    ppermute x15, starting transfers between devices, ctx_shift(): return lax.ppermute(value, 'ctx', pairs)  40.3 us
    ppermute x15, waiting for transfers between devices, ctx_shift(): return lax.ppermute(value, 'ctx', pairs)  37.8 us
    pallas_call x4, Pallas kernels, far_call(): pl.pallas_call(lambda *refs: far_kernel(n, *refs), in_specs=[SMEM, SMEM,...  21.3 us
    pallas_call x2, Pallas kernels, last_call(): pl.pallas_call(lambda *refs: last_kernel(n, aheads, *refs), in_specs=[SME...  9.96 us
    ppermute x7, waiting for transfers between devices, head_shift(): return lax.ppermute(value, 'head', pairs)  9.93 us
    ppermute x7, starting transfers between devices, head_shift(): return lax.ppermute(value, 'head', pairs)  9.69 us
    pallas_call x1, Pallas kernels, serve_call(): pl.pallas_call(lambda *refs: serve_kernel(members, *refs), in_specs=[SMEM...  7.07 us
    pallas_call x1, Pallas kernels, first_call(): pl.pallas_call(lambda *refs: first_kernel(members, heads, *refs), in_spec...  6.24 us
  transfers between devices with their start and end apart: 23, of which 6 were waited for; matrix products, arithmetic and copies ran while one was open for 0% of the time, Pallas kernels for 25%

commit v1 on v0

--- a/solution.py
+++ b/solution.py
@@ -14,6 +14,7 @@
 QB = 4
 ENTRIES = QB * TOPK
 SIDE = 4
+RANGE_BITS = 5
 ONES = 16
 C = DH ** -0.5 * 1.4426950408889634
 
@@ -44,7 +45,7 @@
 
 def ctx_position():
     rank = lax.axis_index("ctx")
-    return rank // SIDE, rank % SIDE
+    return rank >> 2, rank & (SIDE - 1)
 
 
 def serve_start(members, sel_ref, tiles_ref, outs, stage, sem, sem_out):
@@ -53,14 +54,14 @@
     copies = []
     for out, number in zip(outs, members):
         dy, dx = (0, 0) if number == SELF else ORDER[number]
-        asker = ((y + dy) % SIDE) * SIDE + (x + dx) % SIDE
+        asker = ((y + dy) & (SIDE - 1)) * SIDE + ((x + dx) & (SIDE - 1))
         found = jnp.int32(0)
         which = [jnp.int32(0)] * CAP
         for e in range(ENTRIES):
             pick = sel_ref[e % TOPK, 0, asker * QB + e // TOPK]
-            hit = pick // 32 == me
+            hit = pick >> RANGE_BITS == me
             for s in range(CAP):
-                which[s] = jnp.where(hit & (found == s), pick % 32, which[s])
+                which[s] = jnp.where(hit & (found == s), pick & (2 ** RANGE_BITS - 1), which[s])
             found = found + hit.astype(jnp.int32)
         for s in range(CAP):
             place = len(copies)
@@ -197,24 +198,27 @@
     y, x = ctx_position()
     base = (y * SIDE + x) * QB
 
+    def pick_of(e):
+        return sel_ref[lax.rem(e, jnp.int32(TOPK)), 0, base + lax.div(e, jnp.int32(TOPK))]
+
     def fetch(e, found):
-        pick = sel_ref[e % TOPK, 0, base + e // TOPK]
-        owner = pick // 32
-        slot = jnp.int32(0)
-        for f in range(ENTRIES):
-            same = (sel_ref[f % TOPK, 0, base + f // TOPK] // 32 == owner) & (f < e)
-            slot = slot + same.astype(jnp.int32)
-        dy = (y - owner // SIDE + SIDE) % SIDE
-        dx = (x - owner % SIDE + SIDE) % SIDE
+        owner = pick_of(e) >> RANGE_BITS
+        dy = (y - (owner >> 2)) & (SIDE - 1)
+        dx = (x - owner) & (SIDE - 1)
         place = place_ref[dy * SIDE + dx]
-        for i, ref in enumerate(kv_refs):
-            @pl.when(place == i)
-            def _(ref=ref):
-                pltpu.make_async_copy(ref.at[slot], kv_all.at[found], sem.at[found]).start()
 
         @pl.when(place >= 0)
         def _():
-            which_s[found] = e // TOPK
+            slot = jnp.int32(0)
+            for f in range(ENTRIES):
+                same = (pick_of(jnp.int32(f)) >> RANGE_BITS == owner) & (f < e)
+                slot = slot + same.astype(jnp.int32)
+            for i, ref in enumerate(kv_refs):
+                @pl.when(place == i)
+                def _(ref=ref):
+                    pltpu.make_async_copy(ref.at[slot], kv_all.at[found], sem.at[found]).start()
+
+            which_s[found] = lax.div(e, jnp.int32(TOPK))
 
         return found + (place >= 0).astype(jnp.int32)
 
@@ -254,10 +258,10 @@
     acc_in, ml_in, refs = refs[0], refs[1], refs[2:]
     outs, (acc, ml, out_s), scratch = refs[:2 * len(aheads)], refs[2 * len(aheads):][:3], refs[2 * len(aheads) + 3:]
     rank = lax.axis_index("head")
-    core = rank % 2
+    core = rank & 1
     half = BLK // 2
     for i, ahead in enumerate(aheads):
-        b = (rank // 2 + ahead) % QB
+        b = ((rank >> 1) + ahead) & (QB - 1)
         acc[0] = acc_in[b]
         ml[0] = ml_in[b]
         each_arrived(

time: 160 us -> 155 us (0.969); the launches traced: 159 us -> 155 us
  Pallas kernels: 50.4 us -> 46.2 us
  starting transfers between devices: 55.9 us -> 57.9 us
    ppermute x7, starting transfers between devices: 9.69 us -> 15.4 us  [head_shift(): return lax.ppermute(value, 'head', pairs)]
    ppermute x15, starting transfers between devices: 40.3 us -> 36.4 us  [ctx_shift(): return lax.ppermute(value, 'ctx', pairs)]
    pallas_call x4, Pallas kernels: 21.3 us -> 17.6 us  [far_call(): pl.pallas_call(lambda *refs: far_kernel(n, *refs), in_specs=[SMEM, SMEM,...]
    ppermute x7, waiting for transfers between devices: 9.93 us -> 6.96 us  [head_shift(): return lax.ppermute(value, 'head', pairs)]
    ppermute x15, waiting for transfers between devices: 37.8 us -> 40 us  [ctx_shift(): return lax.ppermute(value, 'ctx', pairs)]
  transfers between devices with their start and end apart: 23 -> 23, of which waited for: 6 -> 8; matrix products, arithmetic and copies ran while one was open for 0% -> 0% of each run, Pallas kernels for 25% -> 24%
where the time goes in v1:
time: 155 us
  starting transfers between devices  57.9 us (37%)
  waiting for transfers between devices  46.9 us (30%)
  Pallas kernels  46.2 us (30%)
  local copies, waits for them, and re-layouts  4.16 us (3%)
    ppermute x15, waiting for transfers between devices, ctx_shift(): return lax.ppermute(value, 'ctx', pairs)  40 us
    ppermute x15, starting transfers between devices, ctx_shift(): return lax.ppermute(value, 'ctx', pairs)  36.4 us
    pallas_call x4, Pallas kernels, far_call(): pl.pallas_call(lambda *refs: far_kernel(n, *refs), in_specs=[SMEM, SMEM,...  17.6 us
    ppermute x7, starting transfers between devices, head_shift(): return lax.ppermute(value, 'head', pairs)  15.4 us
    pallas_call x2, Pallas kernels, last_call(): pl.pallas_call(lambda *refs: last_kernel(n, aheads, *refs), in_specs=[SME...  8.95 us
    pallas_call x1, Pallas kernels, serve_call(): pl.pallas_call(lambda *refs: serve_kernel(members, *refs), in_specs=[SMEM...  7.6 us
    ppermute x7, waiting for transfers between devices, head_shift(): return lax.ppermute(value, 'head', pairs)  6.96 us
    pallas_call x1, Pallas kernels, first_call(): pl.pallas_call(lambda *refs: first_kernel(members, heads, *refs), in_spec...  6.19 us
  transfers between devices with their start and end apart: 23, of which 8 were waited for; matrix products, arithmetic and copies ran while one was open for 0% of the time, Pallas kernels for 24%

profile of v1, /device:TPU:25, one launch (start us, length us, event | category | flops | bytes accessed | tf_op | source)
XLA Modules:
  0.0 155.4 jit_solution(559958865583295319)
XLA Ops:
  0.0 6.2 %first.1 = (bf16[2,512,256]{2,1,0:T(8,128)(2,1)}, bf16[2,512,256]{2,1,0:T(8,128)(2,1)}, bf16[2,512,256]{2,1,0:T(8,128)(2,1)}, bf16[2,512,256]{2,1,0:T(8,128)(2,1...) custom-call(s32[3,1,64]{2,1,0:T(1,128)} %bitcast.10, bf16[32,512,256]{2,1,0:T(8,128)(2,1)} %bitcast.18, ...), custom_call_target="tpu_custom_call" | custom-call | tf_op jit(solution)/shard_map/first/pallas_call | solution.py:136
  6.2 6.1 %all-to-all-start = ((bf16[8,256,768]{2,1,0:T(8,128)(2,1)}), bf16[8,256,768]{2,1,0:T(8,128)(2,1)S(1)}, u32[]{:S(2)}, u32[]{:S(2)}) async-start(bf16[8,256,768]{2,1,0:T(8,128)(2,1)} %get-tuple-element.78), calls=%async_computation | async-start | bytes 6291456 | tf_op jit(solution)/shard_map/all_to_all | solution.py:383
  15.0 1.4 collective-permute-start.7
  16.4 2.1 %collective-permute-start.10 = (bf16[2,512,256]{2,1,0:T(8,128)(2,1)}, bf16[2,512,256]{2,1,0:T(8,128)(2,1)S(1)}, u32[]{:S(2)}, u32[]{:S(2)}) collective-permute-start(bf16[2,512,256]{2,1,0:T(8,128)(2,1)} %get-tuple-element.108), channel_id=1, source_target_pairs={{0,80},{8,88},{16,64},{24,72},{32,112},{40,120},{48,96},{56,104},{... | collective-permute-start | bytes 1572872 | tf_op jit(solution)/shard_map/ppermute | solution.py:364
  18.5 7.6 %serve.1 = (bf16[2,512,256]{2,1,0:T(8,128)(2,1)}, bf16[2,512,256]{2,1,0:T(8,128)(2,1)}, bf16[2,512,256]{2,1,0:T(8,128)(2,1)}, bf16[2,512,256]{2,1,0:T(8,128)(2,1...) custom-call(s32[3,1,64]{2,1,0:T(1,128)} %bitcast.11, ...), custom_call_target="tpu_custom_call" | custom-call | tf_op jit(solution)/shard_map/serve/pallas_call | solution.py:122
  29.7 2.8 %collective-permute-start.4 = (bf16[2,512,256]{2,1,0:T(8,128)(2,1)}, bf16[2,512,256]{2,1,0:T(8,128)(2,1)}, u32[]{:S(2)}, u32[]{:S(2)}) collective-permute-start(bf16[2,512,256]{2,1,0:T(8,128)(2,1)} %get-tuple-element.92), channel_id=1, source_target_pairs={{0,120},{8,96},{16,104},{24,112},{32,24},{40,0},{48,8},{56,16},{64... | collective-permute-start | bytes 1572872 | tf_op jit(solution)/shard_map/ppermute | solution.py:364
  33.3 1.4 collective-permute-start.1
  36.5 5.2 %collective-permute-done.10.refs_5_ = bf16[2,512,256]{2,1,0:T(8,128)(2,1)S(1)} collective-permute-done((bf16[2,512,256]{2,1,0:T(8,128)(2,1)}, bf16[2,512,256]{2,1,0:T(8,128)(2,1)S(1)}, u32[]{:S(2)}, u32[]{:S(2)}) %collective-permute-start.10) | collective-permute-done | bytes 524320 | tf_op jit(solution)/shard_map/ppermute | solution.py:364
  42.5 14.2 %collective-permute-start.11 = (bf16[2,512,256]{2,1,0:T(8,128)(2,1)}, bf16[2,512,256]{2,1,0:T(8,128)(2,1)}, u32[]{:S(2)}, u32[]{:S(2)}) collective-permute-start(bf16[2,512,256]{2,1,0:T(8,128)(2,1)} %get-tuple-element.109), channel_id=1, source_target_pairs={{0,48},{8,56},{16,32},{24,40},{32,80},{40,88},{48,64},{56,72},{64,... | collective-permute-start | bytes 1572872 | tf_op jit(solution)/shard_map/ppermute | solution.py:364
  56.7 4.4 %own_blocks.1 = (f32[4,4,128,512]{3,2,1,0:T(8,128)S(1)}, f32[4,4,8,512]{3,2,1,0:T(8,128)S(1)}) custom-call(bf16[4,512,768]{2,1,0:T(8,128)(2,1)S(1)} %bitcast.3), custom_call_target="tpu_custom_call" | custom-call | flops 2147483648 | bytes 2097152 | tf_op jit(solution)/shard_map/own_blocks/pallas_call | solution.py:294
  62.9 2.8 %far_blocks.4 = (f32[4,4,128,512]{3,2,1,0:T(8,128)S(1)}, f32[4,4,8,512]{3,2,1,0:T(8,128)S(1)}) custom-call(s32[3,1,64]{2,1,0:T(1,128)S(1)} %bitcast.12, s32[16]{0:T(128)S(1)} %copy-done.16, bf16[4,512,768]{2,1,0:T(8,128)(2,1)S(1)} %bitcast.4, bf16[2,512,256]{2,1,0:T(8,128)(2,1)S(1)} %copy-done.10, bf16[2,512,256]{2,1,0:T(8,128)(2,1)S(1)} %copy-done.7, ...), custom_call_target="tpu_custom_call" | custom-call | flops 1207959552 | bytes 1179648 | tf_op jit(solution)/shard_map/far_blocks/pallas_call | solution.py:307
  67.0 7.7 %collective-permute-done.11.refs_7_ = bf16[2,512,256]{2,1,0:T(8,128)(2,1)} collective-permute-done((bf16[2,512,256]{2,1,0:T(8,128)(2,1)}, bf16[2,512,256]{2,1,0:T(8,128)(2,1)}, u32[]{:S(2)}, u32[]{:S(2)}) %collective-permute-start.11) | collective-permute-done | bytes 524320 | tf_op jit(solution)/shard_map/ppermute | solution.py:364
  74.7 4.2 %collective-permute-start.12 = (bf16[2,512,256]{2,1,0:T(8,128)(2,1)S(1)}, bf16[2,512,256]{2,1,0:T(8,128)(2,1)S(1)}, u32[]{:S(2)}, u32[]{:S(2)}) collective-permute-start(bf16[2,512,256]{2,1,0:T(8,128)(2,1)S(1)} %copy-done.19), channel_id=1, source_target_pairs={{0,64},{8,72},{16,80},{24,88},{32,96},{40,104},{48,112},{56,120},{... | collective-permute-start | bytes 1572872 | tf_op jit(solution)/shard_map/ppermute | solution.py:364
  79.0 3.6 %collective-permute-start.9 = (bf16[2,512,256]{2,1,0:T(8,128)(2,1)S(1)}, bf16[2,512,256]{2,1,0:T(8,128)(2,1)S(1)}, u32[]{:S(2)}, u32[]{:S(2)}) collective-permute-start(bf16[2,512,256]{2,1,0:T(8,128)(2,1)S(1)} %copy-done.18), channel_id=1, source_target_pairs={{0,16},{8,24},{16,0},{24,8},{32,48},{40,56},{48,32},{56,40},{64,80... | collective-permute-start | bytes 1572872 | tf_op jit(solution)/shard_map/ppermute | solution.py:364
  83.1 7.8 %far_blocks.6 = (f32[4,4,128,512]{3,2,1,0:T(8,128)S(1)}, f32[4,4,8,512]{3,2,1,0:T(8,128)S(1)}) custom-call(s32[3,1,64]{2,1,0:T(1,128)S(1)} %bitcast.14, s32[16]{0:T(128)S(1)} %copy-done.14, bf16[4,512,768]{2,1,0:T(8,128)(2,1)S(1)} %bitcast.6, bf16[2,512,256]{2,1,0:T(8,128)(2,1)} %collective-permute-done.5.refs_3_, ...), custom_call_target="tpu_custom_call" | custom-call | flops 2013265920 | bytes 1966080 | tf_op jit(solution)/shard_map/far_blocks/pallas_call | solution.py:307
  90.9 14.7 %collective-permute-done.13.refs_3_ = bf16[2,512,256]{2,1,0:T(8,128)(2,1)S(1)} collective-permute-done((bf16[2,512,256]{2,1,0:T(8,128)(2,1)S(1)}, bf16[2,512,256]{2,1,0:T(8,128)(2,1)S(1)}, u32[]{:S(2)}, u32[]{:S(2)}) %collective-permute-start.13) | collective-permute-done | bytes 524320 | tf_op jit(solution)/shard_map/ppermute | solution.py:364
  105.6 5.7 %far_blocks.7 = (f32[4,4,128,512]{3,2,1,0:T(8,128)S(1)}, f32[4,4,8,512]{3,2,1,0:T(8,128)S(1)}) custom-call(s32[3,1,64]{2,1,0:T(1,128)S(1)} %bitcast.15, s32[16]{0:T(128)S(1)} %copy-done.13, bf16[4,512,768]{2,1,0:T(8,128)(2,1)S(1)} %bitcast.7, bf16[2,512,256]{2,1,0:T(8,128)(2,1)S(1)} %collective-permute-done.13.refs_3_, ...), custom_call_target="tpu_custom_call" | custom-call | flops 805306368 | bytes 786432 | tf_op jit(solution)/shard_map/far_blocks/pallas_call | solution.py:307
  111.3 11.2 %collective-permute-done.12.refs_5_ = bf16[2,512,256]{2,1,0:T(8,128)(2,1)S(1)} collective-permute-done((bf16[2,512,256]{2,1,0:T(8,128)(2,1)S(1)}, bf16[2,512,256]{2,1,0:T(8,128)(2,1)S(1)}, u32[]{:S(2)}, u32[]{:S(2)}) %collective-permute-start.12) | collective-permute-done | bytes 524320 | tf_op jit(solution)/shard_map/ppermute | solution.py:364
  123.7 9.6 %collective-permute-start.16 = (bf16[256,512]{1,0:T(8,128)(2,1)S(1)}, bf16[256,512]{1,0:T(8,128)(2,1)S(1)}, u32[]{:S(2)}, u32[]{:S(2)}) collective-permute-start(bf16[256,512]{1,0:T(8,128)(2,1)S(1)} %get-tuple-element.143), channel_id=1, source_target_pairs={{0,5},{1,4},{2,7},{3,6},{4,1},{5,0},{6,3},{7,2},{8,13},{9,12},{10,... | collective-permute-start | bytes 786440 | tf_op jit(solution)/shard_map/ppermute | solution.py:369
  133.3 7.9 %last_blocks.3 = (bf16[256,512]{1,0:T(8,128)(2,1)S(1)}, bf16[256,512]{1,0:T(8,128)(2,1)S(1)}, bf16[256,512]{1,0:T(8,128)(2,1)S(1)}, bf16[256,512]{1,0:T(8,128)(2...) custom-call(s32[3,1,64]{2,1,0:T(1,128)S(1)} %bitcast.17, s32[16]{0:T(128)S(1)} %copy-done.12, ...), custom_call_target="tpu_custom_call" | custom-call | flops 536870912 | bytes 524288 | tf_op jit(solution)/shard_map/last_blocks/pallas_call | solution.py:322
  141.3 2.7 %collective-permute-start.18 = (bf16[256,512]{1,0:T(8,128)(2,1)S(1)}, bf16[256,512]{1,0:T(8,128)(2,1)S(1)}, u32[]{:S(2)}, u32[]{:S(2)}) collective-permute-start(bf16[256,512]{1,0:T(8,128)(2,1)S(1)} %get-tuple-element.146), channel_id=1, source_target_pairs={{0,6},{1,7},{2,0},{3,1},{4,2},{5,3},{6,4},{7,5},{8,14},{9,15},{10,... | collective-permute-start | bytes 786440 | tf_op jit(solution)/shard_map/ppermute | solution.py:369
  144.0 3.0 %collective-permute-start.20 = (bf16[256,512]{1,0:T(8,128)(2,1)S(1)}, bf16[256,512]{1,0:T(8,128)(2,1)S(1)}, u32[]{:S(2)}, u32[]{:S(2)}) collective-permute-start(bf16[256,512]{1,0:T(8,128)(2,1)S(1)} %get-tuple-element.148), channel_id=1, source_target_pairs={{0,7},{1,6},{2,1},{3,0},{4,3},{5,2},{6,5},{7,4},{8,15},{9,14},{10,... | collective-permute-start | bytes 786440 | tf_op jit(solution)/shard_map/ppermute | solution.py:369
  149.5 4.4 %collective-permute-done.19.refs_4_ = bf16[256,512]{1,0:T(8,128)(2,1)S(1)} collective-permute-done((bf16[256,512]{1,0:T(8,128)(2,1)S(1)}, bf16[256,512]{1,0:T(8,128)(2,1)S(1)}, u32[]{:S(2)}, u32[]{:S(2)}) %collective-permute-start.19) | collective-permute-done | bytes 262176 | tf_op jit(solution)/shard_map/ppermute | solution.py:369
  153.9 1.5 assemble.1
  (76 shorter events, 16.9 us)
Async XLA Ops:
  6.2 50.5 %all-to-all-start = ((bf16[8,256,768]{2,1,0:T(8,128)(2,1)}), bf16[8,256,768]{2,1,0:T(8,128)(2,1)S(1)}, u32[]{:S(2)}, u32[]{:S(2)}) async-start(bf16[8,256,768]{2,1,0:T(8,128)(2,1)} %get-tuple-element.78), calls=%async_computation | async-start | bytes 6291456 | tf_op jit(solution)/shard_map/all_to_all | solution.py:383
  12.3 15.0 %collective-permute-start.2 = (bf16[2,512,256]{2,1,0:T(8,128)(2,1)}, bf16[2,512,256]{2,1,0:T(8,128)(2,1)S(1)}, u32[]{:S(2)}, u32[]{:S(2)}) collective-permute-start(bf16[2,512,256]{2,1,0:T(8,128)(2,1)} %get-tuple-element.85), channel_id=1, source_target_pairs={{0,8},{8,16},{16,24},{24,0},{32,40},{40,48},{48,56},{56,32},{64,72... | collective-permute-start | bytes 1572872 | tf_op jit(solution)/shard_map/ppermute | solution.py:364
  13.6 15.3 %collective-permute-start.3 = (bf16[2,512,256]{2,1,0:T(8,128)(2,1)}, bf16[2,512,256]{2,1,0:T(8,128)(2,1)S(1)}, u32[]{:S(2)}, u32[]{:S(2)}) collective-permute-start(bf16[2,512,256]{2,1,0:T(8,128)(2,1)} %get-tuple-element.88), channel_id=1, source_target_pairs={{0,24},{8,0},{16,8},{24,16},{32,56},{40,32},{48,40},{56,48},{64,88... | collective-permute-start | bytes 1572872 | tf_op jit(solution)/shard_map/ppermute | solution.py:364
  14.9 17.6 %collective-permute-start = (bf16[2,512,256]{2,1,0:T(8,128)(2,1)}, bf16[2,512,256]{2,1,0:T(8,128)(2,1)S(1)}, u32[]{:S(2)}, u32[]{:S(2)}) collective-permute-start(bf16[2,512,256]{2,1,0:T(8,128)(2,1)} %get-tuple-element.81), channel_id=1, source_target_pairs={{0,32},{8,40},{16,48},{24,56},{32,64},{40,72},{48,80},{56,88},{64,... | collective-permute-start | bytes 1572872 | tf_op jit(solution)/shard_map/ppermute | solution.py:364
  15.0 19.7 %collective-permute-start.7 = (bf16[2,512,256]{2,1,0:T(8,128)(2,1)}, bf16[2,512,256]{2,1,0:T(8,128)(2,1)S(1)}, u32[]{:S(2)}, u32[]{:S(2)}) collective-permute-start(bf16[2,512,256]{2,1,0:T(8,128)(2,1)} %get-tuple-element.102), channel_id=1, source_target_pairs={{0,96},{8,104},{16,112},{24,120},{32,0},{40,8},{48,16},{56,24},{64... | collective-permute-start | bytes 1572872 | tf_op jit(solution)/shard_map/ppermute | solution.py:364
  16.4 25.3 %collective-permute-start.10 = (bf16[2,512,256]{2,1,0:T(8,128)(2,1)}, bf16[2,512,256]{2,1,0:T(8,128)(2,1)S(1)}, u32[]{:S(2)}, u32[]{:S(2)}) collective-permute-start(bf16[2,512,256]{2,1,0:T(8,128)(2,1)} %get-tuple-element.108), channel_id=1, source_target_pairs={{0,80},{8,88},{16,64},{24,72},{32,112},{40,120},{48,96},{56,104},{... | collective-permute-start | bytes 1572872 | tf_op jit(solution)/shard_map/ppermute | solution.py:364
  26.1 36.7 %copy-start.11 = (s32[1,64,3]{1,0,2:T(1,128)S(1)}, s32[1,64,3]{1,0,2:T(1,128)}, u32[]{:S(2)}) copy-start(s32[1,64,3]{1,0,2:T(1,128)} %param.13) | copy-start | bytes 2308
  28.1 33.0 %collective-permute-start.5 = (bf16[2,512,256]{2,1,0:T(8,128)(2,1)}, bf16[2,512,256]{2,1,0:T(8,128)(2,1)}, u32[]{:S(2)}, u32[]{:S(2)}) collective-permute-start(bf16[2,512,256]{2,1,0:T(8,128)(2,1)} %get-tuple-element.94), channel_id=1, source_target_pairs={{0,40},{8,48},{16,56},{24,32},{32,72},{40,80},{48,88},{56,64},{64,... | collective-permute-start | bytes 1572872 | tf_op jit(solution)/shard_map/ppermute | solution.py:364
  29.7 31.4 %collective-permute-start.4 = (bf16[2,512,256]{2,1,0:T(8,128)(2,1)}, bf16[2,512,256]{2,1,0:T(8,128)(2,1)}, u32[]{:S(2)}, u32[]{:S(2)}) collective-permute-start(bf16[2,512,256]{2,1,0:T(8,128)(2,1)} %get-tuple-element.92), channel_id=1, source_target_pairs={{0,120},{8,96},{16,104},{24,112},{32,24},{40,0},{48,8},{56,16},{64... | collective-permute-start | bytes 1572872 | tf_op jit(solution)/shard_map/ppermute | solution.py:364
  33.3 32.4 %collective-permute-start.1 = (bf16[2,512,256]{2,1,0:T(8,128)(2,1)}, bf16[2,512,256]{2,1,0:T(8,128)(2,1)}, u32[]{:S(2)}, u32[]{:S(2)}) collective-permute-start(bf16[2,512,256]{2,1,0:T(8,128)(2,1)} %get-tuple-element.82), channel_id=1, source_target_pairs={{0,56},{8,32},{16,40},{24,48},{32,88},{40,64},{48,72},{56,80},{64,... | collective-permute-start | bytes 1572872 | tf_op jit(solution)/shard_map/ppermute | solution.py:364
  35.5 30.2 %collective-permute-start.8 = (bf16[2,512,256]{2,1,0:T(8,128)(2,1)}, bf16[2,512,256]{2,1,0:T(8,128)(2,1)}, u32[]{:S(2)}, u32[]{:S(2)}) collective-permute-start(bf16[2,512,256]{2,1,0:T(8,128)(2,1)} %get-tuple-element.103), channel_id=1, source_target_pairs={{0,104},{8,112},{16,120},{24,96},{32,8},{40,16},{48,24},{56,0},{64... | collective-permute-start | bytes 1572872 | tf_op jit(solution)/shard_map/ppermute | solution.py:364
  42.5 32.2 %collective-permute-start.11 = (bf16[2,512,256]{2,1,0:T(8,128)(2,1)}, bf16[2,512,256]{2,1,0:T(8,128)(2,1)}, u32[]{:S(2)}, u32[]{:S(2)}) collective-permute-start(bf16[2,512,256]{2,1,0:T(8,128)(2,1)} %get-tuple-element.109), channel_id=1, source_target_pairs={{0,48},{8,56},{16,32},{24,40},{32,80},{40,88},{48,64},{56,72},{64,... | collective-permute-start | bytes 1572872 | tf_op jit(solution)/shard_map/ppermute | solution.py:364
  61.1 29.8 %collective-permute-start.14 = (bf16[2,512,256]{2,1,0:T(8,128)(2,1)S(1)}, bf16[2,512,256]{2,1,0:T(8,128)(2,1)S(1)}, u32[]{:S(2)}, u32[]{:S(2)}) collective-permute-start(bf16[2,512,256]{2,1,0:T(8,128)(2,1)S(1)} %copy-done.21), channel_id=1, source_target_pairs={{0,72},{8,80},{16,88},{24,64},{32,104},{40,112},{48,120},{56,96},{... | collective-permute-start | bytes 1572872 | tf_op jit(solution)/shard_map/ppermute | solution.py:364
  62.4 43.1 %collective-permute-start.13 = (bf16[2,512,256]{2,1,0:T(8,128)(2,1)S(1)}, bf16[2,512,256]{2,1,0:T(8,128)(2,1)S(1)}, u32[]{:S(2)}, u32[]{:S(2)}) collective-permute-start(bf16[2,512,256]{2,1,0:T(8,128)(2,1)S(1)} %copy-done.20), channel_id=1, source_target_pairs={{0,112},{8,120},{16,96},{24,104},{32,16},{40,24},{48,0},{56,8},{64... | collective-permute-start | bytes 1572872 | tf_op jit(solution)/shard_map/ppermute | solution.py:364
  74.7 47.8 %collective-permute-start.12 = (bf16[2,512,256]{2,1,0:T(8,128)(2,1)S(1)}, bf16[2,512,256]{2,1,0:T(8,128)(2,1)S(1)}, u32[]{:S(2)}, u32[]{:S(2)}) collective-permute-start(bf16[2,512,256]{2,1,0:T(8,128)(2,1)S(1)} %copy-done.19), channel_id=1, source_target_pairs={{0,64},{8,72},{16,80},{24,88},{32,96},{40,104},{48,112},{56,120},{... | collective-permute-start | bytes 1572872 | tf_op jit(solution)/shard_map/ppermute | solution.py:364
  79.0 43.6 %collective-permute-start.9 = (bf16[2,512,256]{2,1,0:T(8,128)(2,1)S(1)}, bf16[2,512,256]{2,1,0:T(8,128)(2,1)S(1)}, u32[]{:S(2)}, u32[]{:S(2)}) collective-permute-start(bf16[2,512,256]{2,1,0:T(8,128)(2,1)S(1)} %copy-done.18), channel_id=1, source_target_pairs={{0,16},{8,24},{16,0},{24,8},{32,48},{40,56},{48,32},{56,40},{64,80... | collective-permute-start | bytes 1572872 | tf_op jit(solution)/shard_map/ppermute | solution.py:364
  82.6 39.9 %collective-permute-start.6 = (bf16[2,512,256]{2,1,0:T(8,128)(2,1)S(1)}, bf16[2,512,256]{2,1,0:T(8,128)(2,1)S(1)}, u32[]{:S(2)}, u32[]{:S(2)}) collective-permute-start(bf16[2,512,256]{2,1,0:T(8,128)(2,1)S(1)} %copy-done.17), channel_id=1, source_target_pairs={{0,88},{8,64},{16,72},{24,80},{32,120},{40,96},{48,104},{56,112},{... | collective-permute-start | bytes 1572872 | tf_op jit(solution)/shard_map/ppermute | solution.py:364
  123.6 20.4 %collective-permute-start.15 = (bf16[256,512]{1,0:T(8,128)(2,1)S(1)}, bf16[256,512]{1,0:T(8,128)(2,1)S(1)}, u32[]{:S(2)}, u32[]{:S(2)}) collective-permute-start(bf16[256,512]{1,0:T(8,128)(2,1)S(1)} %get-tuple-element.140), channel_id=1, source_target_pairs={{0,4},{1,5},{2,6},{3,7},{4,0},{5,1},{6,2},{7,3},{8,12},{9,13},{10,... | collective-permute-start | bytes 786440 | tf_op jit(solution)/shard_map/ppermute | solution.py:369
  123.7 23.3 %collective-permute-start.16 = (bf16[256,512]{1,0:T(8,128)(2,1)S(1)}, bf16[256,512]{1,0:T(8,128)(2,1)S(1)}, u32[]{:S(2)}, u32[]{:S(2)}) collective-permute-start(bf16[256,512]{1,0:T(8,128)(2,1)S(1)} %get-tuple-element.143), channel_id=1, source_target_pairs={{0,5},{1,4},{2,7},{3,6},{4,1},{5,0},{6,3},{7,2},{8,13},{9,12},{10,... | collective-permute-start | bytes 786440 | tf_op jit(solution)/shard_map/ppermute | solution.py:369
  141.2 6.9 %collective-permute-start.17 = (bf16[256,512]{1,0:T(8,128)(2,1)S(1)}, bf16[256,512]{1,0:T(8,128)(2,1)S(1)}, u32[]{:S(2)}, u32[]{:S(2)}) collective-permute-start(bf16[256,512]{1,0:T(8,128)(2,1)S(1)} %get-tuple-element.145), channel_id=1, source_target_pairs={{0,2},{1,3},{2,4},{3,5},{4,6},{5,7},{6,0},{7,1},{8,10},{9,11},{10,... | collective-permute-start | bytes 786440 | tf_op jit(solution)/shard_map/ppermute | solution.py:369
  141.3 8.2 %collective-permute-start.18 = (bf16[256,512]{1,0:T(8,128)(2,1)S(1)}, bf16[256,512]{1,0:T(8,128)(2,1)S(1)}, u32[]{:S(2)}, u32[]{:S(2)}) collective-permute-start(bf16[256,512]{1,0:T(8,128)(2,1)S(1)} %get-tuple-element.146), channel_id=1, source_target_pairs={{0,6},{1,7},{2,0},{3,1},{4,2},{5,3},{6,4},{7,5},{8,14},{9,15},{10,... | collective-permute-start | bytes 786440 | tf_op jit(solution)/shard_map/ppermute | solution.py:369
  144.0 9.9 %collective-permute-start.19 = (bf16[256,512]{1,0:T(8,128)(2,1)S(1)}, bf16[256,512]{1,0:T(8,128)(2,1)S(1)}, u32[]{:S(2)}, u32[]{:S(2)}) collective-permute-start(bf16[256,512]{1,0:T(8,128)(2,1)S(1)} %get-tuple-element.147), channel_id=1, source_target_pairs={{0,3},{1,2},{2,5},{3,4},{4,7},{5,6},{6,1},{7,0},{8,11},{9,10},{10,... | collective-permute-start | bytes 786440 | tf_op jit(solution)/shard_map/ppermute | solution.py:369
  144.0 9.9 %collective-permute-start.20 = (bf16[256,512]{1,0:T(8,128)(2,1)S(1)}, bf16[256,512]{1,0:T(8,128)(2,1)S(1)}, u32[]{:S(2)}, u32[]{:S(2)}) collective-permute-start(bf16[256,512]{1,0:T(8,128)(2,1)S(1)} %get-tuple-element.148), channel_id=1, source_target_pairs={{0,7},{1,6},{2,1},{3,0},{4,3},{5,2},{6,5},{7,4},{8,15},{9,14},{10,... | collective-permute-start | bytes 786440 | tf_op jit(solution)/shard_map/ppermute | solution.py:369
  146.9 7.0 %collective-permute-start.21 = (bf16[256,512]{1,0:T(8,128)(2,1)S(1)}, bf16[256,512]{1,0:T(8,128)(2,1)S(1)}, u32[]{:S(2)}, u32[]{:S(2)}) collective-permute-start(bf16[256,512]{1,0:T(8,128)(2,1)S(1)} %get-tuple-element.149), channel_id=1, source_target_pairs={{0,1},{1,0},{2,3},{3,2},{4,5},{5,4},{6,7},{7,6},{8,9},{9,8},{10,11... | collective-permute-start | bytes 786440 | tf_op jit(solution)/shard_map/ppermute | solution.py:369
  (21 other events, 176.7 us)
